TPU v7x, 32 devices: a whole 2x2x4 slice. The times are simulated.
32 devices in a mesh: groups: 2 (over y), space: 4 (over z), dp: 4 (over x, core).
Axes of the slice: x: 2, y: 2, z: 4, core: 2. Of those that a mesh axis runs over, the one named last changes fastest.
Arguments:
- features: bfloat16 [8, 6144, 64], P(('groups', 'dp'), 'space'), parts along dimension 0, may hold values from -6 to 6
- kernel_map: int32 [8, 27, 6144], P(('groups', 'dp'), None, 'space'), parts along dimension 0, may hold values from 0 to 2560, as said below
- child_map: int32 [8, 8, 1536], P(('groups', 'dp'), None, 'space'), parts along dimension 0, may hold values from 0 to 2048, as said below
- live_rows: int32 [8, 4], P(('groups', 'dp'), 'space'), parts along dimension 0, may hold values from 768 to 1536, as said below
- weight_first: bfloat16 [27, 64, 64], replicated, may hold values from -0.15625 to 0.15625
- weight_second: bfloat16 [27, 64, 64], replicated, may hold values from -0.15625 to 0.15625
- weight_down: bfloat16 [8, 64, 128], replicated, may hold values from -0.25 to 0.25
- out_grad: bfloat16 [8, 1536, 128], P(('groups', 'dp'), 'space'), parts along dimension 0, may hold values from -6 to 6
Outputs:
- coarse_features: bfloat16 [8, 1536, 128], P(('groups', 'dp'), 'space'), parts along dimension 0
- feature_grad: bfloat16 [8, 6144, 64], P(('groups', 'dp'), 'space'), parts along dimension 0
- grad_first: bfloat16 [54, 64, 64], P('groups'), parts along dimension 0
- grad_second: bfloat16 [54, 64, 64], P('groups'), parts along dimension 0
- grad_down: bfloat16 [16, 64, 128], P('groups'), parts along dimension 0
There are 2 independent parts, one for each index of `groups`. A program takes and returns all parts, laid end to end along the dimension named above; an argument that names none is the same for every part. Nothing has to cross between parts.
Inputs may be any that keep to these rules, and one draw needn't show every extreme that they name: `kernel_map`: entries equal to 2560 mean no input; offset 27 // 2 of a row below its device's live count reads that row itself; rows at or above the live count read nothing. `child_map`: entries equal to 2048 mean no child; child 0 is present unless it falls past the strip's end. `live_rows`: in every sample some device is full.
All inputs are finite; a program needn't handle non-finite values.
Results may differ from a plain program's by a relative error of at most 0.006.
Values may be sent and summed in bfloat16 or wider, within the bound.
No kernel may reach another device: no remote copies, remote signals or barrier semaphores. Data moves between devices by JAX's collectives and lax.ppermute only.
A program may use at most 128 MiB of HBM per device.

v0:
```python
import functools

import jax
import jax.numpy as jnp
from jax import lax
from jax.experimental import pallas as pl
from jax.experimental.pallas import tpu as pltpu
from jax.sharding import PartitionSpec as P

HALO = 512
READ_SLABS = 2
SPREAD_SPAN = 256
DOWN_SPAN = 512
LOW = 18
ROW = 16
UNROLL = 8
VMEM_BYTES = 24 * 2**20
LIVE, FIRST, LAST, DP = range(4)


def silu_slope(value):
    sig = jax.nn.sigmoid(value)
    return sig * (1.0 + value * (1.0 - sig))


def locate(index, span, count):
    slab = sum((index >= span * s).astype(jnp.int32) for s in range(1, count))
    return slab, jnp.where(index >= 0, index - slab * span, -1)


def one_hot(place, span):
    shape = (span, place.shape[1])
    here = jnp.broadcast_to(place, shape).astype(jnp.int16)
    return jnp.where(
        here == lax.broadcasted_iota(jnp.int16, shape, 0), jnp.bfloat16(1), jnp.bfloat16(0)
    )


def nt(left, right):
    return lax.dot_general(
        left, right, (((1,), (1,)), ((), ())), preferred_element_type=jnp.float32
    )


def nn(left, right):
    return jnp.dot(left, right, preferred_element_type=jnp.float32)


def repeat(step, count):
    rounds, rest = divmod(count, min(UNROLL, max(1, count // 2)))
    steps = (count - rest) // rounds

    def turn(i, carry):
        for u in range(steps):
            step(i * steps + u)
        return carry

    lax.fori_loop(0, rounds, turn, 0)
    for u in range(count - rest, count):
        step(jnp.int32(u))


def read_rows(slabs, index, chans):
    count, span = slabs.shape[0] // chans, slabs.shape[1]
    slab, place = locate(index, span, count)
    read = nn(slabs, one_hot(place, span))
    picked = read[(count - 1) * chans :]
    for s in range(count - 1):
        picked = jnp.where(slab == s, read[s * chans : (s + 1) * chans], picked)
    return picked.astype(jnp.bfloat16)


def spread_rows(terms_ref, terms, index, count, span):
    chans = terms.shape[0]
    slab, place = locate(index, span, count)
    for s in range(count):
        terms_ref[s * chans : (s + 1) * chans, :] = jnp.where(slab == s, terms, jnp.zeros_like(terms))
    return nt(terms_ref[...], one_hot(place, span))


def conv(info_ref, map_ref, weight_ref, slabs_ref, taken_ref, own, blocks):
    count, chans = weight_ref.shape[0], weight_ref.shape[1]
    window = map_ref.shape[2] + 2 * HALO
    centre = count // 2
    alive = live_mask(info_ref, map_ref.shape[2])
    for place, block in enumerate(blocks):
        taken_ref[centre * chans : (centre + 1) * chans, place * HALO : (place + 1) * HALO] = jnp.where(
            alive[:, block * HALO : (block + 1) * HALO], own[block], jnp.zeros_like(own[block])
        )

    def step(i):
        k = i + (i >= centre).astype(jnp.int32)
        index = map_ref[k]
        index = jnp.where(index < window, index, -1)
        at = pl.ds(pl.multiple_of(k * chans, chans), chans)
        for place, block in enumerate(blocks):
            part = index[:, block * HALO : (block + 1) * HALO]
            taken_ref[at, place * HALO : (place + 1) * HALO] = read_rows(slabs_ref[...], part, chans)

    repeat(step, count - 1)
    weights = weight_ref[...].reshape(count * chans, -1).T
    return nn(weights, taken_ref[...])


def conv_back(map_ref, weight_ref, grad_ref, terms_ref, sums_ref, halo, begin, end):
    count, chans = weight_ref.shape[0], weight_ref.shape[1]
    rows = grad_ref.shape[1]
    slabs = sums_ref.shape[0]
    centre = count // 2
    holds = begin <= centre < end

    def step(i):
        k = i + begin
        if holds:
            k += (k >= centre).astype(jnp.int32)
        index = map_ref[k]
        if halo:
            after = (index >= HALO + rows) & (index < 2 * HALO + rows)
            index = jnp.where(after, index - rows, jnp.where(index < HALO, index, -1))
        else:
            index = jnp.where(index < HALO + rows, index - HALO, -1)
        sums = spread_rows(terms_ref, grad_ref[...], index, slabs, SPREAD_SPAN).astype(jnp.bfloat16)
        at = pl.ds(pl.multiple_of((k - begin) * chans, chans), chans)
        for s in range(slabs):
            sums_ref[s, at, :] = sums[s * chans : (s + 1) * chans]

    if holds:
        at = slice((centre - begin) * chans, (centre - begin + 1) * chans)
        for s in range(slabs):
            own = grad_ref[:, s * SPREAD_SPAN : (s + 1) * SPREAD_SPAN]
            sums_ref[s, at, :] = jnp.zeros_like(own) if halo else own
    repeat(step, end - begin - holds)
    weights = jnp.concatenate([weight_ref[k] for k in range(begin, end)], axis=1)
    return [nn(weights, sums_ref[s]) for s in range(slabs)]


def put_window(slabs_ref, info_ref, before, own, after):
    zero = jnp.zeros_like(before)
    before = jnp.where(info_ref[0, FIRST] == 1, zero, before)
    after = jnp.where(info_ref[0, LAST] == 1, zero, after)
    chans, span = before.shape[0], slabs_ref.shape[1]
    at = 0
    for part in [before] + own + [after]:
        done = 0
        while done < part.shape[1]:
            slab, column = divmod(at, span)
            take = min(span - column, part.shape[1] - done)
            slabs_ref[slab * chans : (slab + 1) * chans, column : column + take] = part[
                :, done : done + take
            ]
            done, at = done + take, at + take


def in_parts(ref):
    return [ref[:, at : at + HALO] for at in range(0, ref.shape[1], HALO)]


def ends_around(outer_ref, inner_ref):
    first, last = in_parts(outer_ref)
    return [first] + in_parts(inner_ref) + [last]


def live_mask(info_ref, rows):
    return lax.broadcasted_iota(jnp.int32, (1, rows), 1) < info_ref[0, LIVE]


def add_ends(info_ref, own, before, after):
    rows = own.shape[1]
    before = jnp.where(info_ref[0, FIRST] == 1, 0.0, before.astype(jnp.float32))
    after = jnp.where(info_ref[0, LAST] == 1, 0.0, after.astype(jnp.float32))
    return jnp.concatenate(
        [
            own[:, :HALO] + before,
            own[:, HALO : rows - HALO],
            own[:, rows - HALO :] + after,
        ],
        axis=1,
    )


def spread_kernel(
    child_hbm, down_hbm, grad_hbm, own_ref, next_ref, terms_ref, child_ref, down_ref, grad_ref, sems
):
    copies = [
        pltpu.make_async_copy(source, target, sems.at[i])
        for i, (source, target) in enumerate(
            ((child_hbm, child_ref), (down_hbm, down_ref), (grad_hbm, grad_ref))
        )
    ]
    for copy in copies:
        copy.start()
    for copy in copies:
        copy.wait()
    kids, chans, wide = down_ref.shape
    rows = own_ref.shape[1]
    slabs = (rows + HALO) // DOWN_SPAN
    total = jnp.zeros((slabs * chans, DOWN_SPAN), jnp.float32)
    terms = nt(down_ref[...].reshape(kids * chans, wide), grad_ref[...]).astype(jnp.bfloat16)
    for j in range(kids):
        index = child_ref[j : j + 1, :]
        index = jnp.where(index < rows + HALO, index, -1)
        total += spread_rows(terms_ref, terms[j * chans : (j + 1) * chans], index, slabs, DOWN_SPAN)
    for s in range(slabs - 1):
        own_ref[:, s * DOWN_SPAN : (s + 1) * DOWN_SPAN] = total[s * chans : (s + 1) * chans]
    next_ref[...] = total[(slabs - 1) * chans :].astype(next_ref.dtype)


def first_part(info_ref, map_ref, weight_ref, field_ref, slabs_ref, first_ref, slope_ref, taken_ref, blocks):
    pre = conv(info_ref, map_ref, weight_ref, slabs_ref, taken_ref, in_parts(field_ref), blocks)
    alive = live_mask(info_ref, map_ref.shape[2])
    for place, block in enumerate(blocks):
        part = slice(place * HALO, (place + 1) * HALO)
        lives = alive[:, block * HALO : (block + 1) * HALO]
        value = pre[:, part]
        first_ref[:, part] = jnp.where(lives, jax.nn.silu(value), 0.0).astype(jnp.bfloat16)
        slope_ref[:, part] = jnp.where(lives, silu_slope(value), 0.0)


def outer_kernel(
    info_ref,
    map_ref,
    weight_ref,
    field_ref,
    before_ref,
    after_ref,
    spread_ref,
    first_ref,
    slope_ref,
    taken_ref,
    to_next_ref,
    slabs_ref,
):
    put_window(slabs_ref, info_ref, before_ref[...], in_parts(field_ref), after_ref[...])
    blocks = [0, field_ref.shape[1] // HALO - 1]
    first_part(
        info_ref, map_ref, weight_ref, field_ref, slabs_ref, first_ref, slope_ref, taken_ref, blocks
    )
    chans = field_ref.shape[0]
    to_next_ref[:chans] = first_ref[:, HALO:]
    to_next_ref[chans:] = spread_ref[...]


def inner_kernel(
    info_ref,
    map_ref,
    weight_ref,
    field_ref,
    before_ref,
    after_ref,
    first_ref,
    slope_ref,
    taken_ref,
    slabs_ref,
):
    put_window(slabs_ref, info_ref, before_ref[...], in_parts(field_ref), after_ref[...])
    blocks = list(range(1, field_ref.shape[1] // HALO - 1))
    first_part(
        info_ref, map_ref, weight_ref, field_ref, slabs_ref, first_ref, slope_ref, taken_ref, blocks
    )


def second_kernel(
    info_ref,
    map_ref,
    weight_ref,
    outer_ref,
    inner_ref,
    before_ref,
    after_ref,
    field_ref,
    rows_ref,
    second_ref,
    d_second_ref,
    grad_weight_ref,
    to_prev_ref,
    to_next_ref,
    slabs_ref,
    taken_ref,
    terms_ref,
    sums_ref,
):
    chans, rows = field_ref.shape
    own = ends_around(outer_ref, inner_ref)
    put_window(slabs_ref, info_ref, before_ref[:chans], own, after_ref[...])
    blocks = list(range(rows // HALO))
    pre = conv(info_ref, map_ref, weight_ref, slabs_ref, taken_ref, own, blocks) + field_ref[...].astype(jnp.float32)
    alive = live_mask(info_ref, rows)
    second_ref[...] = jnp.where(alive, jax.nn.silu(pre), 0.0).astype(jnp.bfloat16)
    slope = jnp.where(alive, silu_slope(pre), 0.0)
    returned = jnp.where(info_ref[0, FIRST] == 1, 0.0, before_ref[chans:].astype(jnp.float32))
    grad_rows = jnp.concatenate([rows_ref[:, :HALO] + returned, rows_ref[:, HALO:]], axis=1)
    d_second_ref[...] = (grad_rows * slope).astype(jnp.bfloat16)
    grad_weight_ref[...] = nt(d_second_ref[...], taken_ref[...])
    ends = conv_back(
        map_ref, weight_ref, d_second_ref, terms_ref, sums_ref, True, 0, map_ref.shape[0]
    )
    half = len(ends) // 2
    to_prev_ref[:chans] = jnp.concatenate(ends[:half], axis=1).astype(to_prev_ref.dtype)
    to_prev_ref[chans:] = second_ref[:, :HALO]
    to_next_ref[...] = jnp.concatenate(ends[half:], axis=1).astype(to_next_ref.dtype)


def own_kernel(begin, end, map_ref, weight_ref, grad_ref, own_ref, terms_ref, sums_ref):
    parts = conv_back(map_ref, weight_ref, grad_ref, terms_ref, sums_ref, False, begin, end)
    for s, part in enumerate(parts):
        own_ref[:, s * SPREAD_SPAN : (s + 1) * SPREAD_SPAN] = part


def low_kernel(
    begin, end, map_ref, weight_ref, grad_ref, kids_ref, down_ref, own_ref, coarse_ref, terms_ref, sums_ref
):
    own_kernel(begin, end, map_ref, weight_ref, grad_ref, own_ref, terms_ref, sums_ref)
    kids, chans, wide = down_ref.shape
    flat = down_ref[...].reshape(kids * chans, wide)
    coarse_ref[...] = nn(kids_ref[...].T, flat).astype(jnp.bfloat16)


def ends_kernel(map_ref, weight_ref, grad_ref, to_prev_ref, to_next_ref, terms_ref, sums_ref):
    ends = conv_back(map_ref, weight_ref, grad_ref, terms_ref, sums_ref, True, 0, map_ref.shape[0])
    half = len(ends) // 2
    for ref, parts in ((to_prev_ref, ends[:half]), (to_next_ref, ends[half:])):
        stack_to_row(ref, jnp.concatenate(parts, axis=1).astype(ref.dtype))


def stack_to_row(ref, value):
    group, width = ref.shape[0], value.shape[1]
    for i in range(value.shape[0] // group):
        ref[:, i * width : (i + 1) * width] = value[i * group : (i + 1) * group]


def row_to_stack(ref, chans):
    width = ref.shape[1] * ref.shape[0] // chans
    return jnp.concatenate([ref[:, i : i + width] for i in range(0, ref.shape[1], width)], axis=0)


def middle_kernel(
    info_ref,
    child_ref,
    down_ref,
    grad_ref,
    second_ref,
    from_next_ref,
    from_prev_ref,
    rows_ref,
    slope_outer_ref,
    slope_inner_ref,
    taken_outer_ref,
    taken_inner_ref,
    grad_second_ref,
    d_first_ref,
    grads_ref,
    kids_ref,
    slabs_ref,
):
    kids, chans, wide = down_ref.shape
    rows = second_ref.shape[1]
    for s in range(rows // DOWN_SPAN):
        slabs_ref[s * chans : (s + 1) * chans, :] = second_ref[:, s * DOWN_SPAN : (s + 1) * DOWN_SPAN]
    after = from_next_ref[chans:]
    slabs_ref[rows // DOWN_SPAN * chans :, :] = jnp.where(
        info_ref[0, LAST] == 1, jnp.zeros_like(after), after
    )
    for j in range(kids):
        index = child_ref[j : j + 1, :]
        index = jnp.where(index < rows + HALO, index, -1)
        kids_ref[j * chans : (j + 1) * chans, :] = read_rows(slabs_ref[...], index, chans)
    grad_down = nn(kids_ref[...], grad_ref[...])
    slope = jnp.concatenate(ends_around(slope_outer_ref, slope_inner_ref), axis=1)
    d_first = (
        add_ends(info_ref, rows_ref[...], from_prev_ref[...], from_next_ref[:chans]) * slope
    ).astype(jnp.bfloat16)
    d_first_ref[...] = d_first
    d_outer = jnp.concatenate([d_first[:, :HALO], d_first[:, rows - HALO :]], axis=1)
    size = grad_second_ref.shape[1]
    grads_ref[:, :size] = grad_second_ref[...]
    grads_ref[:, size : 2 * size] = nt(d_outer, taken_outer_ref[...]) + nt(
        d_first[:, HALO : rows - HALO], taken_inner_ref[...]
    )
    for j in range(kids):
        grads_ref[:, 2 * size + j * wide : 2 * size + (j + 1) * wide] = grad_down[
            j * chans : (j + 1) * chans
        ]


def last_kernel(info_ref, low_ref, high_ref, d_second_ref, before_ref, after_ref, *refs):
    quarters, (field_ref, first_ref, second_ref, down_ref, grads_ref) = refs[:-5], refs[-5:]
    chans = low_ref.shape[0]
    before, after = row_to_stack(before_ref, chans), row_to_stack(after_ref, chans)
    total = add_ends(info_ref, low_ref[...] + high_ref[...], before, after)
    field_ref[...] = (total + d_second_ref[...].astype(jnp.float32)).astype(jnp.bfloat16)
    share = quarters[0].shape[0]
    for step, quarter_ref in enumerate(quarters):
        at = (info_ref[0, DP] ^ step) * share if len(quarters) > 1 else 0
        grads_ref[pl.ds(pl.multiple_of(at, ROW), share), :] = quarter_ref[...]
    count = first_ref.shape[0]
    kids, wide = down_ref.shape[0], down_ref.shape[2]
    size = count * chans
    second = grads_ref[:, :size].T
    first = grads_ref[:, size : 2 * size].T
    for k in range(count):
        second_ref[k] = second[k * chans : (k + 1) * chans]
        first_ref[k] = first[k * chans : (k + 1) * chans]
    for j in range(kids):
        down_ref[j] = grads_ref[:, 2 * size + j * wide : 2 * size + (j + 1) * wide]


def shape(dims, dtype):
    return jax.ShapeDtypeStruct(dims, dtype)


def call(kernel, outs, scratch, flops, *args, where=pltpu.VMEM, limit=VMEM_BYTES):
    smem = pl.BlockSpec(memory_space=pltpu.SMEM)
    vmem = pl.BlockSpec(memory_space=pltpu.VMEM)
    return pl.pallas_call(
        kernel,
        out_shape=outs,
        in_specs=[smem if a.shape == (1, 4) else pl.BlockSpec(memory_space=where) for a in args],
        out_specs=[vmem] * len(outs),
        scratch_shapes=scratch,
        compiler_params=pltpu.CompilerParams(vmem_limit_bytes=limit),
        cost_estimate=pl.CostEstimate(flops=flops, bytes_accessed=2**20, transcendentals=0),
    )(*args)


def shifted(value, axis, steps):
    count = lax.axis_size(axis)
    return lax.ppermute(value, axis, [(i, (i + steps) % count) for i in range(count)])


def body(
    features, kernel_map, child_map, live_rows, weight_first, weight_second, weight_down, out_grad
):
    bf16, f32 = jnp.bfloat16, jnp.float32
    field = features[0].T
    chans, rows = field.shape
    count = kernel_map.shape[1]
    offsets = kernel_map.reshape(count, 1, rows)
    children = child_map[0]
    kids, coarse = children.shape
    wide = weight_down.shape[2]
    grad_out = out_grad[0]
    place = lax.axis_index("space")
    devices = lax.axis_size("space")
    info = jnp.stack(
        [
            live_rows[0, 0],
            (place == 0).astype(jnp.int32),
            (place == devices - 1).astype(jnp.int32),
            lax.axis_index("dp").astype(jnp.int32),
        ]
    ).reshape(1, 4)
    window = rows + 2 * HALO
    flops = 2 * count * window * chans * rows
    down_slabs = (rows + HALO) // DOWN_SPAN
    slabs_scratch = pltpu.VMEM((READ_SLABS * chans, window // READ_SLABS), bf16)

    def back_scratch(width, offset_count):
        slabs = width // SPREAD_SPAN
        return [
            pltpu.VMEM((slabs * chans, rows), bf16),
            pltpu.VMEM((slabs, offset_count * chans, SPREAD_SPAN), bf16),
        ]

    before = shifted(field[:, rows - HALO :], "space", 1)
    after = shifted(field[:, :HALO], "space", -1)
    grad_rows, spread_next = call(
        spread_kernel,
        [shape((chans, rows), f32), shape((chans, HALO), bf16)],
        [
            pltpu.VMEM((down_slabs * chans, coarse), bf16),
            pltpu.VMEM(children.shape, jnp.int32),
            pltpu.VMEM(weight_down.shape, bf16),
            pltpu.VMEM(grad_out.shape, bf16),
            pltpu.SemaphoreType.DMA((3,)),
        ],
        2 * kids * (rows + HALO) * chans * coarse,
        children,
        weight_down,
        grad_out,
        where=pltpu.HBM,
        limit=60 * 2**20,
    )
    first_outer, slope_outer, taken_outer, to_next = call(
        outer_kernel,
        [
            shape((chans, 2 * HALO), bf16),
            shape((chans, 2 * HALO), f32),
            shape((count * chans, 2 * HALO), bf16),
            shape((2 * chans, HALO), bf16),
        ],
        [slabs_scratch],
        flops * 2 // 3,
        info,
        offsets,
        weight_first,
        field,
        before,
        after,
        spread_next,
    )
    before, after, first_outer, to_next = lax.optimization_barrier((before, after, first_outer, to_next))
    first_inner, slope_inner, taken_inner = call(
        inner_kernel,
        [
            shape((chans, rows - 2 * HALO), bf16),
            shape((chans, rows - 2 * HALO), f32),
            shape((count * chans, rows - 2 * HALO), bf16),
        ],
        [slabs_scratch],
        flops // 3,
        info,
        offsets,
        weight_first,
        field,
        before,
        after,
    )
    before = shifted(to_next, "space", 1)
    after = shifted(first_outer[:, :HALO], "space", -1)
    second, d_second, grad_second, to_prev, to_next = call(
        second_kernel,
        [
            shape((chans, rows), bf16),
            shape((chans, rows), bf16),
            shape((chans, count * chans), f32),
            shape((2 * chans, HALO), bf16),
            shape((chans, HALO), bf16),
        ],
        [slabs_scratch, pltpu.VMEM((count * chans, rows), bf16)]
        + back_scratch(2 * HALO, count),
        flops * 3 // 2,
        info,
        offsets,
        weight_second,
        first_outer,
        first_inner,
        before,
        after,
        field,
        grad_rows,
    )
    from_next = shifted(to_prev, "space", -1)
    from_prev = shifted(to_next, "space", 1)
    (own,) = call(
        functools.partial(own_kernel, 0, count),
        [shape((chans, rows), f32)],
        back_scratch(rows, count),
        flops // 2,
        offsets,
        weight_second,
        d_second,
    )
    d_first, grads, kid_rows = call(
        middle_kernel,
        [
            shape((chans, rows), bf16),
            shape((chans, 2 * count * chans + kids * wide), f32),
            shape((kids * chans, coarse), bf16),
        ],
        [pltpu.VMEM((down_slabs * chans, DOWN_SPAN), bf16)],
        2 * kids * (rows + HALO) * chans * coarse,
        info,
        children,
        weight_down,
        grad_out,
        second,
        from_next,
        from_prev,
        own,
        slope_outer,
        slope_inner,
        taken_outer,
        taken_inner,
        grad_second,
    )
    samples = lax.axis_size("dp")
    direct = samples == 4 and devices == 4 and chans // samples == ROW
    scale = float(samples * devices * rows) ** (-0.5)
    me = lax.axis_index("dp")
    share = chans // samples

    def partner(value, step):
        return lax.ppermute(value, "dp", [(i, i ^ step) for i in range(samples)])

    def quarter(step):
        return lax.dynamic_slice_in_dim(grads, (me ^ step) * share, share, axis=0)

    if direct:
        sent = [quarter(s).astype(bf16) for s in range(1, samples)]
        sent, d_first = lax.optimization_barrier((sent, d_first))
        got = [partner(v, s + 1) for s, v in enumerate(sent)]
    to_prev, to_next = call(
        ends_kernel,
        [shape((ROW, chans // ROW * HALO), bf16), shape((ROW, chans // ROW * HALO), bf16)],
        back_scratch(2 * HALO, count),
        flops // 2,
        offsets,
        weight_first,
        d_first,
    )
    if direct:
        got, to_prev, to_next = lax.optimization_barrier((got, to_prev, to_next))
        sent = (quarter(0) + sum(v.astype(f32) for v in got)).astype(bf16)
        sent, d_first = lax.optimization_barrier((sent, d_first))
        forth = shifted(jnp.concatenate([sent, to_next], axis=1), "space", 1)
        back = shifted(jnp.concatenate([sent, to_prev], axis=1), "space", -1)
        across = shifted(sent, "space", 2)
    else:
        after = shifted(to_prev, "space", -1)
        before = shifted(to_next, "space", 1)
    low, coarse_out = call(
        functools.partial(low_kernel, 0, LOW),
        [shape((chans, rows), f32), shape((coarse, wide), bf16)],
        back_scratch(rows, LOW),
        flops // 3,
        offsets,
        weight_first,
        d_first,
        kid_rows,
        weight_down,
    )
    if direct:
        forth, back, across, low = lax.optimization_barrier((forth, back, across, low))
        width = grads.shape[1]
        before, after = forth[:, width:], back[:, width:]
        even = sent.astype(f32) + across.astype(f32)
        odd = forth[:, :width].astype(f32) + back[:, :width].astype(f32)
        part = ((even + odd) * scale).astype(bf16)
        part, d_first = lax.optimization_barrier((part, d_first))
        parts = [part, partner(part, 1), partner(part, 2)]
    (high,) = call(
        functools.partial(own_kernel, LOW, count),
        [shape((chans, rows), f32)],
        back_scratch(rows, count - LOW),
        flops // 6,
        offsets,
        weight_first,
        d_first,
    )
    if direct:
        parts, high = lax.optimization_barrier((parts, high))
        parts.append(partner(parts[2], 1))
    else:
        parts = [(lax.psum(grads, ("space", "dp")) * scale).astype(bf16)]
    feature_grad, out_first, out_second, out_down = call(
        last_kernel,
        [
            shape((chans, rows), bf16),
            shape(weight_first.shape, bf16),
            shape(weight_second.shape, bf16),
            shape(weight_down.shape, bf16),
        ],
        [pltpu.VMEM(grads.shape, bf16)],
        1,
        info,
        low,
        high,
        d_second,
        before,
        after,
        *parts,
    )
    return (coarse_out[None], feature_grad.T[None], out_first, out_second, out_down)


def solution(mesh):
    placed = (
        P(("groups", "dp"), "space", None),
        P(("groups", "dp"), None, "space"),
        P(("groups", "dp"), None, "space"),
        P(("groups", "dp"), "space"),
        P(),
        P(),
        P(),
        P(("groups", "dp"), "space", None),
    )
    return jax.shard_map(
        body,
        mesh=mesh,
        in_specs=placed,
        out_specs=(
            P(("groups", "dp"), "space", None),
            P(("groups", "dp"), "space", None),
            P("groups", None, None),
            P("groups", None, None),
            P("groups", None, None),
        ),
        check_vma=False,
    )
```

profile of v0, /device:TPU:0, one launch (start us, length us, event | category | flops | bytes accessed | tf_op | source)
XLA Modules:
  0.0 107.6 jit_solution(6426503396989168757)
XLA Ops:
  0.6 0.9 fusion
  1.5 3.1 %collective-permute-start = (bf16[64,512]{1,0:T(8,128)(2,1)S(1)}, bf16[64,512]{1,0:T(8,128)(2,1)S(1)}, u32[]{:S(2)}, u32[]{:S(2)}) collective-permute-start(bf16[64,512]{1,0:T(8,128)(2,1)S(1)} %get-tuple-element.109), channel_id=1, source_target_pairs={{0,4},{4,8},{8,12},{12,0},{1,5},{5,9},{9,13},{13,1},{2,6},{6,10},{... | collective-permute-start | bytes 196616 | tf_op jit(solution)/shard_map/ppermute | solution.py:427
  4.6 2.1 %collective-permute-start.1 = (bf16[64,512]{1,0:T(8,128)(2,1)S(1)}, bf16[64,512]{1,0:T(8,128)(2,1)S(1)}, u32[]{:S(2)}, u32[]{:S(2)}) collective-permute-start(bf16[64,512]{1,0:T(8,128)(2,1)S(1)} %get-tuple-element.108), channel_id=1, source_target_pairs={{0,12},{4,0},{8,4},{12,8},{1,13},{5,1},{9,5},{13,9},{2,14},{6,2},{... | collective-permute-start | bytes 196616 | tf_op jit(solution)/shard_map/ppermute | solution.py:427
  7.3 0.1 add_bitcast_fusion.info_ref
  7.4 3.4 %shard_map.119 = (f32[64,1536]{1,0:T(8,128)}, bf16[64,512]{1,0:T(8,128)(2,1)}) custom-call(s32[8,384]{1,0:T(8,128)} %bitcast.23, bf16[8,64,128]{2,1,0:T(8,128)(2,1)} %down_ref.3, bf16[384,128]{1,0:T(8,128)(2,1)} %bitcast.17), custom_call_target="tpu_custom_call" | custom-call | flops 805306368 | bytes 1048576 | tf_op jit(solution)/shard_map/pallas_call | solution.py:414
  10.8 0.0 collective-permute-done.before_ref
  10.8 0.0 collective-permute-done.1.after_ref
  10.9 0.0 copy-start.8
  10.9 0.8 copy-done.8
  11.7 10.8 %shard_map.120 = (bf16[64,1024]{1,0:T(8,128)(2,1)S(1)}, f32[64,1024]{1,0:T(8,128)S(1)}, bf16[1728,1024]{1,0:T(8,128)(2,1)S(1)}, bf16[128,512]{1,0:T(8,128)(2,1)S(1)}) custom-call(s32[1,4]{1,0:T(1,128)S(1)} %add_bitcast_fusion.info_ref, s32[27,1,1536]{2,1,0:T(1,128)S(1)} %bitcast.25, bf16[27,64,64]{2,1,0:T(8,128)(2,1)S(1)} %copy-done.5, ...), custom_call_target="tpu_custom_call" | custom-call | flops 9059696640 | bytes 1048576 | tf_op jit(solution)/shard_map/pallas_call | solution.py:414
  22.5 0.0 copy-start.4
  22.5 0.0 copy-start.7
  22.5 2.0 %collective-permute-start.3 = (bf16[64,512]{1,0:T(8,128)(2,1)S(1)}, bf16[64,512]{1,0:T(8,128)(2,1)S(1)}, u32[]{:S(2)}, u32[]{:S(2)}) collective-permute-start(bf16[64,512]{1,0:T(8,128)(2,1)S(1)} %slice.23), channel_id=1, source_target_pairs={{0,12},{4,0},{8,4},{12,8},{1,13},{5,1},{9,5},{13,9},{2,14},{6,2},{... | collective-permute-start | bytes 196616 | tf_op jit(solution)/shard_map/ppermute | solution.py:427
  24.6 0.1 collective-permute-start.2
  24.6 6.0 %shard_map.121 = (bf16[64,512]{1,0:T(8,128)(2,1)S(1)}, f32[64,512]{1,0:T(8,128)S(1)}, bf16[1728,512]{1,0:T(8,128)(2,1)S(1)}) custom-call(s32[1,4]{1,0:T(1,128)S(1)} %add_bitcast_fusion.info_ref, s32[27,1,1536]{2,1,0:T(1,128)S(1)} %bitcast.26, bf16[27,64,64]{2,1,0:T(8,128)(2,1)S(1)} %copy-done.5, bf16[64,1536]{1,0:T(8,128)(2,1)S(1)} %bitcast.21, ...), custom_call_target="tpu_custom_call" | custom-call | flops 4529848320 | bytes 1048576 | tf_op jit(solution)/shard_map/pallas_call | solution.py:414
  30.7 0.0 collective-permute-done.3.after_ref
  30.7 0.6 collective-permute-done.2.before_ref
  31.3 23.6 %shard_map.122 = (bf16[64,1536]{1,0:T(8,128)(2,1)S(1)}, bf16[64,1536]{1,0:T(8,128)(2,1)S(1)}, f32[64,1728]{1,0:T(8,128)S(1)}, bf16[128,512]{1,0:T(8,128)(2,1)S(1)}, bf16[64,512]{1,0:T(8,128)(2,1)S(1)}) custom-call(s32[1,4]{1,0:T(1,128)S(1)} %add_bitcast_fusion.info_ref, s32[27,1,1536]{2,1,0:T(1,128)S(1)} %bitcast.27, bf16[27,64,64]{2,1,0:T(8,128)(2,1)S(1)} %copy-done.4, ...), custom_call_target="tpu_custom_call" | custom-call | flops 20384317440 | bytes 1048576 | tf_op jit(solution)/shard_map/pallas_call | solution.py:414
  55.0 3.2 %collective-permute-start.4 = (bf16[128,512]{1,0:T(8,128)(2,1)S(1)}, bf16[128,512]{1,0:T(8,128)(2,1)S(1)}, u32[]{:S(2)}, u32[]{:S(2)}) collective-permute-start(bf16[128,512]{1,0:T(8,128)(2,1)S(1)} %get-tuple-element.65), channel_id=1, source_target_pairs={{0,12},{4,0},{8,4},{12,8},{1,13},{5,1},{9,5},{13,9},{2,14},{6,2},{... | collective-permute-start | bytes 393224 | tf_op jit(solution)/shard_map/ppermute | solution.py:427
  58.2 0.0 collective-permute-start.5
  58.2 9.9 %shard_map.123.rows_ref = f32[64,1536]{1,0:T(8,128)S(1)} custom-call(s32[27,1,1536]{2,1,0:T(1,128)S(1)} %bitcast.28, bf16[27,64,64]{2,1,0:T(8,128)(2,1)S(1)} %copy-done.4, bf16[64,1536]{1,0:T(8,128)(2,1)S(1)} %get-tuple-element.67.grad_ref.d_second_ref), custom_call_target="tpu_custom_call" | custom-call | flops 6794772480 | bytes 1048576 | tf_op jit(solution)/shard_map/pallas_call | solution.py:414
  68.1 0.0 collective-permute-done.5.from_prev_ref
  68.1 0.0 collective-permute-done.4.from_next_ref
  68.2 3.5 %shard_map.124 = (bf16[64,1536]{1,0:T(8,128)(2,1)S(1)}, f32[64,4480]{1,0:T(8,128)S(1)}, bf16[512,384]{1,0:T(8,128)(2,1)S(1)}) custom-call(s32[1,4]{1,0:T(1,128)S(1)} %add_bitcast_fusion.info_ref, s32[8,384]{1,0:T(8,128)S(1)} %bitcast.24, bf16[8,64,128]{2,1,0:T(8,128)(2,1)S(1)} %copy-done, bf16[384,128]{1,0:T(8,128)(2,1)S(1)} %bitcast.18, ...), custom_call_target="tpu_custom_call" | custom-call | flops 805306368 | bytes 1048576 | tf_op jit(solution)/shard_map/pallas_call | solution.py:414
  71.7 0.1 dynamic-slice_convert_fusion
  71.7 0.1 collective-permute-start.6
  71.8 1.6 %collective-permute-start.7 = (bf16[16,4480]{1,0:T(8,128)(2,1)S(1)}, bf16[16,4480]{1,0:T(8,128)(2,1)S(1)}, u32[]{:S(2)}, u32[]{:S(2)}) collective-permute-start(bf16[16,4480]{1,0:T(8,128)(2,1)S(1)} %get-tuple-element.76), channel_id=1, source_target_pairs={{0,2},{1,3},{2,0},{3,1},{4,6},{5,7},{6,4},{7,5},{8,10},{9,11},{10,... | collective-permute-start | bytes 430088 | tf_op jit(solution)/shard_map/ppermute | solution.py:583
  73.5 0.2 collective-permute-start.8
  73.7 6.8 %shard_map.125 = (bf16[16,2048]{1,0:T(8,128)(2,1)S(1)}, bf16[16,2048]{1,0:T(8,128)(2,1)S(1)}) custom-call(s32[27,1,1536]{2,1,0:T(1,128)S(1)} %bitcast.29, bf16[27,64,64]{2,1,0:T(8,128)(2,1)S(1)} %copy-done.5, bf16[64,1536]{1,0:T(8,128)(2,1)S(1)} %get-tuple-element.96.grad_ref), custom_call_target="tpu_custom_call" | custom-call | flops 6794772480 | bytes 1048576 | tf_op jit(solution)/shard_map/pallas_call | solution.py:414
  80.5 0.0 collective-permute-done.6
  80.5 0.0 collective-permute-done.7
  80.5 0.1 collective-permute-done.8
  80.6 0.1 add_convert_fusion
  80.7 0.9 collective-permute-start.11
  81.6 3.0 %collective-permute-start.10 = (bf16[16,6528]{1,0:T(8,128)(2,1)S(1)}, bf16[16,6528]{1,0:T(8,128)(2,1)S(1)}, u32[]{:S(2)}, u32[]{:S(2)}) collective-permute-start(bf16[16,6528]{1,0:T(8,128)(2,1)S(1)} %get-tuple-element.110), channel_id=1, source_target_pairs={{0,12},{4,0},{8,4},{12,8},{1,13},{5,1},{9,5},{13,9},{2,14},{6,2},{... | collective-permute-start | bytes 626696 | tf_op jit(solution)/shard_map/ppermute | solution.py:427
  84.7 0.9 collective-permute-start.9
  85.5 7.8 %shard_map.126 = (f32[64,1536]{1,0:T(8,128)S(1)}, bf16[384,128]{1,0:T(8,128)(2,1)}) custom-call(s32[27,1,1536]{2,1,0:T(1,128)S(1)} %bitcast.30, bf16[27,64,64]{2,1,0:T(8,128)(2,1)S(1)} %copy-done.5, bf16[64,1536]{1,0:T(8,128)(2,1)S(1)} %get-tuple-element.96.grad_ref, bf16[512,384]{1,0:T(8,128)(2,1)S(1)} %get-tuple-element.85.kids_ref, ...), custom_call_target="tpu_custom_call" | custom-call | flops 4529848320 | bytes 1048576 | tf_op jit(solution)/shard_map/pallas_call | solution.py:414
  93.3 0.0 collective-permute-done.11
  93.3 0.0 collective-permute-done.10
  93.3 4.5 %collective-permute-done.9 = bf16[16,6528]{1,0:T(8,128)(2,1)S(1)} collective-permute-done((bf16[16,6528]{1,0:T(8,128)(2,1)S(1)}, bf16[16,6528]{1,0:T(8,128)(2,1)S(1)}, u32[]{:S(2)}, u32[]{:S(2)}) %collective-permute-start.9) | collective-permute-done | bytes 208928 | tf_op jit(solution)/shard_map/ppermute | solution.py:427
  97.9 0.1 multiply_convert_fusion.refs_0_
  98.0 0.1 collective-permute-start.12
  98.0 1.6 %collective-permute-start.13 = (bf16[16,4480]{1,0:T(8,128)(2,1)S(1)}, bf16[16,4480]{1,0:T(8,128)(2,1)S(1)}, u32[]{:S(2)}, u32[]{:S(2)}) collective-permute-start(bf16[16,4480]{1,0:T(8,128)(2,1)S(1)} %multiply_convert_fusion.refs_0_), channel_id=1, source_target_pairs={{0,2},{1,3},{2,0},{3,1},{4,6},{5,7},{6,4},{7,5},{8,10},{9,11},{10,... | collective-permute-start | bytes 430088 | tf_op jit(solution)/shard_map/ppermute | solution.py:583
  99.7 4.2 %shard_map.127.high_ref = f32[64,1536]{1,0:T(8,128)S(1)} custom-call(s32[27,1,1536]{2,1,0:T(1,128)S(1)} %bitcast.31, bf16[27,64,64]{2,1,0:T(8,128)(2,1)S(1)} %copy-done.5, bf16[64,1536]{1,0:T(8,128)(2,1)S(1)} %get-tuple-element.96.grad_ref), custom_call_target="tpu_custom_call" | custom-call | flops 2264924160 | bytes 1048576 | tf_op jit(solution)/shard_map/pallas_call | solution.py:414
  103.9 0.0 collective-permute-done.12.refs_1_
  103.9 0.3 collective-permute-done.13.refs_2_
  104.3 1.3 %collective-permute-done.14.refs_3_ = bf16[16,4480]{1,0:T(8,128)(2,1)S(1)} collective-permute-done((bf16[16,4480]{1,0:T(8,128)(2,1)S(1)}, bf16[16,4480]{1,0:T(8,128)(2,1)S(1)}, u32[]{:S(2)}, u32[]{:S(2)}) %collective-permute-start.14) | collective-permute-done | bytes 143392 | tf_op jit(solution)/shard_map/ppermute | solution.py:583
  105.6 2.0 %shard_map.128 = (bf16[64,1536]{1,0:T(8,128)(2,1)}, bf16[27,64,64]{2,1,0:T(8,128)(2,1)}, bf16[27,64,64]{2,1,0:T(8,128)(2,1)}, bf16[8,64,128]{2,1,0:T(8,128)(2,1)}) custom-call(s32[1,4]{1,0:T(1,128)S(1)} %add_bitcast_fusion.info_ref, f32[64,1536]{1,0:T(8,128)S(1)} %get-tuple-element.91.low_ref, f32[64,1536]{1,0:T(8,128)S(1)} %shard_map.127.high_ref, ...), custom_call_target="tpu_custom_call" | custom-call | flops 1 | bytes 1048576 | tf_op jit(solution)/shard_map/pallas_call | solution.py:414
  (19 shorter events, 0.1 us)
Async XLA Ops:
  1.5 9.3 %collective-permute-start = (bf16[64,512]{1,0:T(8,128)(2,1)S(1)}, bf16[64,512]{1,0:T(8,128)(2,1)S(1)}, u32[]{:S(2)}, u32[]{:S(2)}) collective-permute-start(bf16[64,512]{1,0:T(8,128)(2,1)S(1)} %get-tuple-element.109), channel_id=1, source_target_pairs={{0,4},{4,8},{8,12},{12,0},{1,5},{5,9},{9,13},{13,1},{2,6},{6,10},{... | collective-permute-start | bytes 196616 | tf_op jit(solution)/shard_map/ppermute | solution.py:427
  4.6 6.2 %collective-permute-start.1 = (bf16[64,512]{1,0:T(8,128)(2,1)S(1)}, bf16[64,512]{1,0:T(8,128)(2,1)S(1)}, u32[]{:S(2)}, u32[]{:S(2)}) collective-permute-start(bf16[64,512]{1,0:T(8,128)(2,1)S(1)} %get-tuple-element.108), channel_id=1, source_target_pairs={{0,12},{4,0},{8,4},{12,8},{1,13},{5,1},{9,5},{13,9},{2,14},{6,2},{... | collective-permute-start | bytes 196616 | tf_op jit(solution)/shard_map/ppermute | solution.py:427
  7.4 3.4 %copy-start.2 = (bf16[1,1536,64]{1,2,0:T(8,128)(2,1)S(1)}, bf16[1,1536,64]{1,2,0:T(8,128)(2,1)}, u32[]{:S(2)}) copy-start(bf16[1,1536,64]{1,2,0:T(8,128)(2,1)} %param.8) | copy-start | bytes 589828
  7.4 3.4 %copy-start.5 = (bf16[27,64,64]{2,1,0:T(8,128)(2,1)S(1)}, bf16[27,64,64]{2,1,0:T(8,128)(2,1)}, u32[]{:S(2)}) copy-start(bf16[27,64,64]{2,1,0:T(8,128)(2,1)} %weight_ref.13) | copy-start | bytes 663556
  7.4 3.4 %copy-start.6 = (s32[1,27,1536]{2,0,1:T(1,128)S(1)}, s32[1,27,1536]{2,0,1:T(1,128)}, u32[]{:S(2)}) copy-start(s32[1,27,1536]{2,0,1:T(1,128)} %param.9) | copy-start | bytes 497668
  10.9 0.8 copy-start.8
  22.5 8.8 %copy-start.4 = (bf16[27,64,64]{2,1,0:T(8,128)(2,1)S(1)}, bf16[27,64,64]{2,1,0:T(8,128)(2,1)}, u32[]{:S(2)}) copy-start(bf16[27,64,64]{2,1,0:T(8,128)(2,1)} %weight_ref.10) | copy-start | bytes 663556
  22.5 8.8 %copy-start.7 = (f32[64,1536]{1,0:T(8,128)S(1)}, f32[64,1536]{1,0:T(8,128)}, u32[]{:S(2)}) copy-start(f32[64,1536]{1,0:T(8,128)} %get-tuple-element.63.rows_ref) | copy-start | bytes 1179652
  22.5 8.1 %collective-permute-start.3 = (bf16[64,512]{1,0:T(8,128)(2,1)S(1)}, bf16[64,512]{1,0:T(8,128)(2,1)S(1)}, u32[]{:S(2)}, u32[]{:S(2)}) collective-permute-start(bf16[64,512]{1,0:T(8,128)(2,1)S(1)} %slice.23), channel_id=1, source_target_pairs={{0,12},{4,0},{8,4},{12,8},{1,13},{5,1},{9,5},{13,9},{2,14},{6,2},{... | collective-permute-start | bytes 196616 | tf_op jit(solution)/shard_map/ppermute | solution.py:427
  24.6 6.8 %collective-permute-start.2 = (bf16[128,512]{1,0:T(8,128)(2,1)S(1)}, bf16[128,512]{1,0:T(8,128)(2,1)S(1)}, u32[]{:S(2)}, u32[]{:S(2)}) collective-permute-start(bf16[128,512]{1,0:T(8,128)(2,1)S(1)} %get-tuple-element.62), channel_id=1, source_target_pairs={{0,4},{4,8},{8,12},{12,0},{1,5},{5,9},{9,13},{13,1},{2,6},{6,10},{... | collective-permute-start | bytes 393224 | tf_op jit(solution)/shard_map/ppermute | solution.py:427
  55.0 13.2 %collective-permute-start.4 = (bf16[128,512]{1,0:T(8,128)(2,1)S(1)}, bf16[128,512]{1,0:T(8,128)(2,1)S(1)}, u32[]{:S(2)}, u32[]{:S(2)}) collective-permute-start(bf16[128,512]{1,0:T(8,128)(2,1)S(1)} %get-tuple-element.65), channel_id=1, source_target_pairs={{0,12},{4,0},{8,4},{12,8},{1,13},{5,1},{9,5},{13,9},{2,14},{6,2},{... | collective-permute-start | bytes 393224 | tf_op jit(solution)/shard_map/ppermute | solution.py:427
  58.2 9.9 %collective-permute-start.5 = (bf16[64,512]{1,0:T(8,128)(2,1)S(1)}, bf16[64,512]{1,0:T(8,128)(2,1)S(1)}, u32[]{:S(2)}, u32[]{:S(2)}) collective-permute-start(bf16[64,512]{1,0:T(8,128)(2,1)S(1)} %get-tuple-element.66), channel_id=1, source_target_pairs={{0,4},{4,8},{8,12},{12,0},{1,5},{5,9},{9,13},{13,1},{2,6},{6,10},{... | collective-permute-start | bytes 196616 | tf_op jit(solution)/shard_map/ppermute | solution.py:427
  58.2 10.0 %copy-start = (bf16[8,64,128]{2,1,0:T(8,128)(2,1)S(1)}, bf16[8,64,128]{2,1,0:T(8,128)(2,1)}, u32[]{:S(2)}) copy-start(bf16[8,64,128]{2,1,0:T(8,128)(2,1)} %down_ref.3) | copy-start | bytes 393220
  58.2 10.0 %copy-start.1 = (bf16[1,384,128]{2,1,0:T(8,128)(2,1)S(1)}, bf16[1,384,128]{2,1,0:T(8,128)(2,1)}, u32[]{:S(2)}) copy-start(bf16[1,384,128]{2,1,0:T(8,128)(2,1)} %param.15) | copy-start | bytes 294916
  58.2 10.0 %copy-start.3 = (s32[1,8,384]{2,1,0:T(8,128)S(1)}, s32[1,8,384]{2,1,0:T(8,128)}, u32[]{:S(2)}) copy-start(s32[1,8,384]{2,1,0:T(8,128)} %param.10) | copy-start | bytes 36868
  71.7 8.8 %collective-permute-start.6 = (bf16[16,4480]{1,0:T(8,128)(2,1)S(1)}, bf16[16,4480]{1,0:T(8,128)(2,1)S(1)}, u32[]{:S(2)}, u32[]{:S(2)}) collective-permute-start(bf16[16,4480]{1,0:T(8,128)(2,1)S(1)} %get-tuple-element.75), channel_id=1, source_target_pairs={{0,1},{1,0},{2,3},{3,2},{4,5},{5,4},{6,7},{7,6},{8,9},{9,8},{10,11... | collective-permute-start | bytes 430088 | tf_op jit(solution)/shard_map/ppermute | solution.py:583
  71.8 8.7 %collective-permute-start.7 = (bf16[16,4480]{1,0:T(8,128)(2,1)S(1)}, bf16[16,4480]{1,0:T(8,128)(2,1)S(1)}, u32[]{:S(2)}, u32[]{:S(2)}) collective-permute-start(bf16[16,4480]{1,0:T(8,128)(2,1)S(1)} %get-tuple-element.76), channel_id=1, source_target_pairs={{0,2},{1,3},{2,0},{3,1},{4,6},{5,7},{6,4},{7,5},{8,10},{9,11},{10,... | collective-permute-start | bytes 430088 | tf_op jit(solution)/shard_map/ppermute | solution.py:583
  73.5 7.2 %collective-permute-start.8 = (bf16[16,4480]{1,0:T(8,128)(2,1)S(1)}, bf16[16,4480]{1,0:T(8,128)(2,1)S(1)}, u32[]{:S(2)}, u32[]{:S(2)}) collective-permute-start(bf16[16,4480]{1,0:T(8,128)(2,1)S(1)} %get-tuple-element.77), channel_id=1, source_target_pairs={{0,3},{1,2},{2,1},{3,0},{4,7},{5,6},{6,5},{7,4},{8,11},{9,10},{10,... | collective-permute-start | bytes 430088 | tf_op jit(solution)/shard_map/ppermute | solution.py:583
  80.7 12.7 %collective-permute-start.11 = (bf16[16,4480]{1,0:T(8,128)(2,1)S(1)}, bf16[16,4480]{1,0:T(8,128)(2,1)S(1)}, u32[]{:S(2)}, u32[]{:S(2)}) collective-permute-start(bf16[16,4480]{1,0:T(8,128)(2,1)S(1)} %add_convert_fusion), channel_id=1, source_target_pairs={{0,8},{4,12},{8,0},{12,4},{1,9},{5,13},{9,1},{13,5},{2,10},{6,14},... | collective-permute-start | bytes 430088 | tf_op jit(solution)/shard_map/ppermute | solution.py:427
  81.6 11.7 %collective-permute-start.10 = (bf16[16,6528]{1,0:T(8,128)(2,1)S(1)}, bf16[16,6528]{1,0:T(8,128)(2,1)S(1)}, u32[]{:S(2)}, u32[]{:S(2)}) collective-permute-start(bf16[16,6528]{1,0:T(8,128)(2,1)S(1)} %get-tuple-element.110), channel_id=1, source_target_pairs={{0,12},{4,0},{8,4},{12,8},{1,13},{5,1},{9,5},{13,9},{2,14},{6,2},{... | collective-permute-start | bytes 626696 | tf_op jit(solution)/shard_map/ppermute | solution.py:427
  84.7 13.2 %collective-permute-start.9 = (bf16[16,6528]{1,0:T(8,128)(2,1)S(1)}, bf16[16,6528]{1,0:T(8,128)(2,1)S(1)}, u32[]{:S(2)}, u32[]{:S(2)}) collective-permute-start(bf16[16,6528]{1,0:T(8,128)(2,1)S(1)} %get-tuple-element.111), channel_id=1, source_target_pairs={{0,4},{4,8},{8,12},{12,0},{1,5},{5,9},{9,13},{13,1},{2,6},{6,10},{... | collective-permute-start | bytes 626696 | tf_op jit(solution)/shard_map/ppermute | solution.py:427
  98.0 6.0 %collective-permute-start.12 = (bf16[16,4480]{1,0:T(8,128)(2,1)S(1)}, bf16[16,4480]{1,0:T(8,128)(2,1)S(1)}, u32[]{:S(2)}, u32[]{:S(2)}) collective-permute-start(bf16[16,4480]{1,0:T(8,128)(2,1)S(1)} %multiply_convert_fusion.refs_0_), channel_id=1, source_target_pairs={{0,1},{1,0},{2,3},{3,2},{4,5},{5,4},{6,7},{7,6},{8,9},{9,8},{10,11... | collective-permute-start | bytes 430088 | tf_op jit(solution)/shard_map/ppermute | solution.py:583
  98.0 6.2 %collective-permute-start.13 = (bf16[16,4480]{1,0:T(8,128)(2,1)S(1)}, bf16[16,4480]{1,0:T(8,128)(2,1)S(1)}, u32[]{:S(2)}, u32[]{:S(2)}) collective-permute-start(bf16[16,4480]{1,0:T(8,128)(2,1)S(1)} %multiply_convert_fusion.refs_0_), channel_id=1, source_target_pairs={{0,2},{1,3},{2,0},{3,1},{4,6},{5,7},{6,4},{7,5},{8,10},{9,11},{10,... | collective-permute-start | bytes 430088 | tf_op jit(solution)/shard_map/ppermute | solution.py:583
  104.2 1.4 %collective-permute-start.14 = (bf16[16,4480]{1,0:T(8,128)(2,1)S(1)}, bf16[16,4480]{1,0:T(8,128)(2,1)S(1)}, u32[]{:S(2)}, u32[]{:S(2)}) collective-permute-start(bf16[16,4480]{1,0:T(8,128)(2,1)S(1)} %collective-permute-done.13.refs_2_), channel_id=1, source_target_pairs={{0,1},{1,0},{2,3},{3,2},{4,5},{5,4},{6,7},{7,6},{8,9},{9,8},{10,11... | collective-permute-start | bytes 430088 | tf_op jit(solution)/shard_map/ppermute | solution.py:583
where the time goes:
time: 108 us
  Pallas kernels  78.2 us (72%)
  starting transfers between devices  18.9 us (17%)
  waiting for transfers between devices  6.92 us (6%)
  local copies, waits for them, and re-layouts  1.84 us (2%)
  between operations  1.56 us (1%)
    pallas_call x10, Pallas kernels, call(): pl.pallas_call(kernel, out_shape=outs, in_specs=[smem if a.shape == (1, 4...  78.2 us
    ppermute x9, starting transfers between devices, shifted(): lax.ppermute(value, axis, [(i, (i + steps) % count) for i in range(count)])  15.3 us
    ppermute x9, waiting for transfers between devices, shifted(): lax.ppermute(value, axis, [(i, (i + steps) % count) for i in range(count)])  5.19 us
    ppermute x6, starting transfers between devices, partner(): return lax.ppermute(value, 'dp', [(i, i ^ step) for i in range(samples)])  3.64 us
  transfers between devices with their start and end apart: 15, of which 5 were waited for; matrix products, arithmetic and copies ran while one was open for 0% of the time, Pallas kernels for 36%

commit v1 on v0

--- a/solution.py
+++ b/solution.py
@@ -382,17 +382,20 @@
         ]
 
 
-def last_kernel(info_ref, low_ref, high_ref, d_second_ref, before_ref, after_ref, *refs):
-    quarters, (field_ref, first_ref, second_ref, down_ref, grads_ref) = refs[:-5], refs[-5:]
+def field_kernel(info_ref, low_ref, high_ref, d_second_ref, before_ref, after_ref, field_ref):
     chans = low_ref.shape[0]
     before, after = row_to_stack(before_ref, chans), row_to_stack(after_ref, chans)
     total = add_ends(info_ref, low_ref[...] + high_ref[...], before, after)
     field_ref[...] = (total + d_second_ref[...].astype(jnp.float32)).astype(jnp.bfloat16)
+
+
+def last_kernel(info_ref, *refs):
+    quarters, (first_ref, second_ref, down_ref, grads_ref) = refs[:-4], refs[-4:]
     share = quarters[0].shape[0]
     for step, quarter_ref in enumerate(quarters):
         at = (info_ref[0, DP] ^ step) * share if len(quarters) > 1 else 0
         grads_ref[pl.ds(pl.multiple_of(at, ROW), share), :] = quarter_ref[...]
-    count = first_ref.shape[0]
+    count, chans = first_ref.shape[0], first_ref.shape[1]
     kids, wide = down_ref.shape[0], down_ref.shape[2]
     size = count * chans
     second = grads_ref[:, :size].T
@@ -642,10 +645,21 @@
         parts.append(partner(parts[2], 1))
     else:
         parts = [(lax.psum(grads, ("space", "dp")) * scale).astype(bf16)]
-    feature_grad, out_first, out_second, out_down = call(
+    (feature_grad,) = call(
+        field_kernel,
+        [shape((chans, rows), bf16)],
+        [],
+        chans * rows,
+        info,
+        low,
+        high,
+        d_second,
+        before,
+        after,
+    )
+    out_first, out_second, out_down = call(
         last_kernel,
         [
-            shape((chans, rows), bf16),
             shape(weight_first.shape, bf16),
             shape(weight_second.shape, bf16),
             shape(weight_down.shape, bf16),
@@ -653,11 +667,6 @@
         [pltpu.VMEM(grads.shape, bf16)],
         1,
         info,
-        low,
-        high,
-        d_second,
-        before,
-        after,
         *parts,
     )
     return (coarse_out[None], feature_grad.T[None], out_first, out_second, out_down)

time: 108 us -> 108 us (level)
  waiting for transfers between devices: 6.92 us -> 5.59 us
    ppermute x6, waiting for transfers between devices: 1.72 us -> 0.39 us  [partner(): return lax.ppermute(value, 'dp', [(i, i ^ step) for i in range(samples)])]
    pallas_call x10 -> x11, Pallas kernels: 78.2 us -> 79.2 us  [call(): pl.pallas_call(kernel, out_shape=outs, in_specs=[smem if a.shape == (1, 4...]
  transfers between devices with their start and end apart: 15 -> 15, of which waited for: 5 -> 4; matrix products, arithmetic and copies ran while one was open for 0% -> 0% of each run, Pallas kernels for 36% -> 37%
where the time goes in v1:
time: 108 us; the launch traced here: 107 us
  Pallas kernels  79.2 us (73%)
  starting transfers between devices  18.9 us (17%)
  waiting for transfers between devices  5.59 us (5%)
  local copies, waits for them, and re-layouts  1.84 us (2%)
  between operations  1.56 us (1%)
    pallas_call x11, Pallas kernels, call(): pl.pallas_call(kernel, out_shape=outs, in_specs=[smem if a.shape == (1, 4...  79.2 us
    ppermute x9, starting transfers between devices, shifted(): lax.ppermute(value, axis, [(i, (i + steps) % count) for i in range(count)])  15.3 us
    ppermute x9, waiting for transfers between devices, shifted(): lax.ppermute(value, axis, [(i, (i + steps) % count) for i in range(count)])  5.2 us
    ppermute x6, starting transfers between devices, partner(): return lax.ppermute(value, 'dp', [(i, i ^ step) for i in range(samples)])  3.64 us
  transfers between devices with their start and end apart: 15, of which 4 were waited for; matrix products, arithmetic and copies ran while one was open for 0% of the time, Pallas kernels for 37%

profile of v1, /device:TPU:0, one launch (start us, length us, event | category | flops | bytes accessed | tf_op | source)
XLA Modules:
  0.0 107.4 jit_solution(11439606413140449137)
XLA Ops:
  0.6 0.9 fusion
  1.5 3.1 %collective-permute-start = (bf16[64,512]{1,0:T(8,128)(2,1)S(1)}, bf16[64,512]{1,0:T(8,128)(2,1)S(1)}, u32[]{:S(2)}, u32[]{:S(2)}) collective-permute-start(bf16[64,512]{1,0:T(8,128)(2,1)S(1)} %get-tuple-element.107), channel_id=1, source_target_pairs={{0,4},{4,8},{8,12},{12,0},{1,5},{5,9},{9,13},{13,1},{2,6},{6,10},{... | collective-permute-start | bytes 196616 | tf_op jit(solution)/shard_map/ppermute | solution.py:430
  4.6 2.1 %collective-permute-start.1 = (bf16[64,512]{1,0:T(8,128)(2,1)S(1)}, bf16[64,512]{1,0:T(8,128)(2,1)S(1)}, u32[]{:S(2)}, u32[]{:S(2)}) collective-permute-start(bf16[64,512]{1,0:T(8,128)(2,1)S(1)} %get-tuple-element.106), channel_id=1, source_target_pairs={{0,12},{4,0},{8,4},{12,8},{1,13},{5,1},{9,5},{13,9},{2,14},{6,2},{... | collective-permute-start | bytes 196616 | tf_op jit(solution)/shard_map/ppermute | solution.py:430
  7.3 0.1 add_bitcast_fusion.info_ref
  7.4 3.4 %shard_map.119 = (f32[64,1536]{1,0:T(8,128)}, bf16[64,512]{1,0:T(8,128)(2,1)}) custom-call(s32[8,384]{1,0:T(8,128)} %bitcast.23, bf16[8,64,128]{2,1,0:T(8,128)(2,1)} %down_ref.3, bf16[384,128]{1,0:T(8,128)(2,1)} %bitcast.17), custom_call_target="tpu_custom_call" | custom-call | flops 805306368 | bytes 1048576 | tf_op jit(solution)/shard_map/pallas_call | solution.py:417
  10.8 0.0 collective-permute-done.before_ref
  10.8 0.0 collective-permute-done.1.after_ref
  10.9 0.0 copy-start.8
  10.9 0.8 copy-done.8
  11.7 10.8 %shard_map.120 = (bf16[64,1024]{1,0:T(8,128)(2,1)S(1)}, f32[64,1024]{1,0:T(8,128)S(1)}, bf16[1728,1024]{1,0:T(8,128)(2,1)S(1)}, bf16[128,512]{1,0:T(8,128)(2,1)S(1)}) custom-call(s32[1,4]{1,0:T(1,128)S(1)} %add_bitcast_fusion.info_ref, s32[27,1,1536]{2,1,0:T(1,128)S(1)} %bitcast.25, bf16[27,64,64]{2,1,0:T(8,128)(2,1)S(1)} %copy-done.5, ...), custom_call_target="tpu_custom_call" | custom-call | flops 9059696640 | bytes 1048576 | tf_op jit(solution)/shard_map/pallas_call | solution.py:417
  22.5 0.0 copy-start.4
  22.5 0.0 copy-start.7
  22.5 2.0 %collective-permute-start.3 = (bf16[64,512]{1,0:T(8,128)(2,1)S(1)}, bf16[64,512]{1,0:T(8,128)(2,1)S(1)}, u32[]{:S(2)}, u32[]{:S(2)}) collective-permute-start(bf16[64,512]{1,0:T(8,128)(2,1)S(1)} %slice.23), channel_id=1, source_target_pairs={{0,12},{4,0},{8,4},{12,8},{1,13},{5,1},{9,5},{13,9},{2,14},{6,2},{... | collective-permute-start | bytes 196616 | tf_op jit(solution)/shard_map/ppermute | solution.py:430
  24.6 0.1 collective-permute-start.2
  24.6 6.0 %shard_map.121 = (bf16[64,512]{1,0:T(8,128)(2,1)S(1)}, f32[64,512]{1,0:T(8,128)S(1)}, bf16[1728,512]{1,0:T(8,128)(2,1)S(1)}) custom-call(s32[1,4]{1,0:T(1,128)S(1)} %add_bitcast_fusion.info_ref, s32[27,1,1536]{2,1,0:T(1,128)S(1)} %bitcast.26, bf16[27,64,64]{2,1,0:T(8,128)(2,1)S(1)} %copy-done.5, bf16[64,1536]{1,0:T(8,128)(2,1)S(1)} %bitcast.21, ...), custom_call_target="tpu_custom_call" | custom-call | flops 4529848320 | bytes 1048576 | tf_op jit(solution)/shard_map/pallas_call | solution.py:417
  30.7 0.0 collective-permute-done.3.after_ref
  30.7 0.6 collective-permute-done.2.before_ref
  31.3 23.6 %shard_map.122 = (bf16[64,1536]{1,0:T(8,128)(2,1)S(1)}, bf16[64,1536]{1,0:T(8,128)(2,1)S(1)}, f32[64,1728]{1,0:T(8,128)S(1)}, bf16[128,512]{1,0:T(8,128)(2,1)S(1)}, bf16[64,512]{1,0:T(8,128)(2,1)S(1)}) custom-call(s32[1,4]{1,0:T(1,128)S(1)} %add_bitcast_fusion.info_ref, s32[27,1,1536]{2,1,0:T(1,128)S(1)} %bitcast.27, bf16[27,64,64]{2,1,0:T(8,128)(2,1)S(1)} %copy-done.4, ...), custom_call_target="tpu_custom_call" | custom-call | flops 20384317440 | bytes 1048576 | tf_op jit(solution)/shard_map/pallas_call | solution.py:417
  55.0 3.2 %collective-permute-start.4 = (bf16[128,512]{1,0:T(8,128)(2,1)S(1)}, bf16[128,512]{1,0:T(8,128)(2,1)S(1)}, u32[]{:S(2)}, u32[]{:S(2)}) collective-permute-start(bf16[128,512]{1,0:T(8,128)(2,1)S(1)} %get-tuple-element.64), channel_id=1, source_target_pairs={{0,12},{4,0},{8,4},{12,8},{1,13},{5,1},{9,5},{13,9},{2,14},{6,2},{... | collective-permute-start | bytes 393224 | tf_op jit(solution)/shard_map/ppermute | solution.py:430
  58.2 0.0 collective-permute-start.5
  58.2 9.9 %shard_map.123.rows_ref = f32[64,1536]{1,0:T(8,128)S(1)} custom-call(s32[27,1,1536]{2,1,0:T(1,128)S(1)} %bitcast.28, bf16[27,64,64]{2,1,0:T(8,128)(2,1)S(1)} %copy-done.4, bf16[64,1536]{1,0:T(8,128)(2,1)S(1)} %get-tuple-element.66.grad_ref.d_second_ref), custom_call_target="tpu_custom_call" | custom-call | flops 6794772480 | bytes 1048576 | tf_op jit(solution)/shard_map/pallas_call | solution.py:417
  68.1 0.0 collective-permute-done.5.from_prev_ref
  68.1 0.0 collective-permute-done.4.from_next_ref
  68.2 3.5 %shard_map.124 = (bf16[64,1536]{1,0:T(8,128)(2,1)S(1)}, f32[64,4480]{1,0:T(8,128)S(1)}, bf16[512,384]{1,0:T(8,128)(2,1)S(1)}) custom-call(s32[1,4]{1,0:T(1,128)S(1)} %add_bitcast_fusion.info_ref, s32[8,384]{1,0:T(8,128)S(1)} %bitcast.24, bf16[8,64,128]{2,1,0:T(8,128)(2,1)S(1)} %copy-done, bf16[384,128]{1,0:T(8,128)(2,1)S(1)} %bitcast.18, ...), custom_call_target="tpu_custom_call" | custom-call | flops 805306368 | bytes 1048576 | tf_op jit(solution)/shard_map/pallas_call | solution.py:417
  71.7 0.1 dynamic-slice_convert_fusion
  71.7 0.1 collective-permute-start.6
  71.8 1.6 %collective-permute-start.7 = (bf16[16,4480]{1,0:T(8,128)(2,1)S(1)}, bf16[16,4480]{1,0:T(8,128)(2,1)S(1)}, u32[]{:S(2)}, u32[]{:S(2)}) collective-permute-start(bf16[16,4480]{1,0:T(8,128)(2,1)S(1)} %get-tuple-element.75), channel_id=1, source_target_pairs={{0,2},{1,3},{2,0},{3,1},{4,6},{5,7},{6,4},{7,5},{8,10},{9,11},{10,... | collective-permute-start | bytes 430088 | tf_op jit(solution)/shard_map/ppermute | solution.py:586
  73.4 0.2 collective-permute-start.8
  73.7 6.8 %shard_map.125 = (bf16[16,2048]{1,0:T(8,128)(2,1)S(1)}, bf16[16,2048]{1,0:T(8,128)(2,1)S(1)}) custom-call(s32[27,1,1536]{2,1,0:T(1,128)S(1)} %bitcast.29, bf16[27,64,64]{2,1,0:T(8,128)(2,1)S(1)} %copy-done.5, bf16[64,1536]{1,0:T(8,128)(2,1)S(1)} %get-tuple-element.95.grad_ref), custom_call_target="tpu_custom_call" | custom-call | flops 6794772480 | bytes 1048576 | tf_op jit(solution)/shard_map/pallas_call | solution.py:417
  80.5 0.0 collective-permute-done.6
  80.5 0.0 collective-permute-done.7
  80.5 0.1 collective-permute-done.8
  80.6 0.1 add_convert_fusion
  80.7 0.9 collective-permute-start.11
  81.6 3.0 %collective-permute-start.10 = (bf16[16,6528]{1,0:T(8,128)(2,1)S(1)}, bf16[16,6528]{1,0:T(8,128)(2,1)S(1)}, u32[]{:S(2)}, u32[]{:S(2)}) collective-permute-start(bf16[16,6528]{1,0:T(8,128)(2,1)S(1)} %get-tuple-element.108), channel_id=1, source_target_pairs={{0,12},{4,0},{8,4},{12,8},{1,13},{5,1},{9,5},{13,9},{2,14},{6,2},{... | collective-permute-start | bytes 626696 | tf_op jit(solution)/shard_map/ppermute | solution.py:430
  84.6 0.9 collective-permute-start.9
  85.5 7.8 %shard_map.126 = (f32[64,1536]{1,0:T(8,128)S(1)}, bf16[384,128]{1,0:T(8,128)(2,1)}) custom-call(s32[27,1,1536]{2,1,0:T(1,128)S(1)} %bitcast.30, bf16[27,64,64]{2,1,0:T(8,128)(2,1)S(1)} %copy-done.5, bf16[64,1536]{1,0:T(8,128)(2,1)S(1)} %get-tuple-element.95.grad_ref, bf16[512,384]{1,0:T(8,128)(2,1)S(1)} %get-tuple-element.84.kids_ref, ...), custom_call_target="tpu_custom_call" | custom-call | flops 4529848320 | bytes 1048576 | tf_op jit(solution)/shard_map/pallas_call | solution.py:417
  93.3 4.5 %collective-permute-done.9 = bf16[16,6528]{1,0:T(8,128)(2,1)S(1)} collective-permute-done((bf16[16,6528]{1,0:T(8,128)(2,1)S(1)}, bf16[16,6528]{1,0:T(8,128)(2,1)S(1)}, u32[]{:S(2)}, u32[]{:S(2)}) %collective-permute-start.9) | collective-permute-done | bytes 208928 | tf_op jit(solution)/shard_map/ppermute | solution.py:430
  97.9 0.1 multiply_convert_fusion.refs_0_
  98.0 0.1 collective-permute-start.12
  98.0 1.6 %collective-permute-start.13 = (bf16[16,4480]{1,0:T(8,128)(2,1)S(1)}, bf16[16,4480]{1,0:T(8,128)(2,1)S(1)}, u32[]{:S(2)}, u32[]{:S(2)}) collective-permute-start(bf16[16,4480]{1,0:T(8,128)(2,1)S(1)} %multiply_convert_fusion.refs_0_), channel_id=1, source_target_pairs={{0,2},{1,3},{2,0},{3,1},{4,6},{5,7},{6,4},{7,5},{8,10},{9,11},{10,... | collective-permute-start | bytes 430088 | tf_op jit(solution)/shard_map/ppermute | solution.py:586
  99.7 4.2 %shard_map.127.high_ref = f32[64,1536]{1,0:T(8,128)S(1)} custom-call(s32[27,1,1536]{2,1,0:T(1,128)S(1)} %bitcast.31, bf16[27,64,64]{2,1,0:T(8,128)(2,1)S(1)} %copy-done.5, bf16[64,1536]{1,0:T(8,128)(2,1)S(1)} %get-tuple-element.95.grad_ref), custom_call_target="tpu_custom_call" | custom-call | flops 2264924160 | bytes 1048576 | tf_op jit(solution)/shard_map/pallas_call | solution.py:417
  103.9 0.0 collective-permute-done.12.refs_1_
  103.9 0.3 collective-permute-done.13.refs_2_
  104.2 0.0 collective-permute-start.14
  104.2 1.3 %shard_map.128 = bf16[64,1536]{1,0:T(8,128)(2,1)} custom-call(s32[1,4]{1,0:T(1,128)S(1)} %add_bitcast_fusion.info_ref, f32[64,1536]{1,0:T(8,128)S(1)} %get-tuple-element.90.low_ref, f32[64,1536]{1,0:T(8,128)S(1)} %shard_map.127.high_ref, bf16[64,1536]{1,0:T(8,128)(2,1)S(1)} %get-tuple-element.66.grad_ref.d_second_ref, ...), custom_call_target="tpu_custom_call" | custom-call | flops 98304 | bytes 1048576 | tf_op jit(solution)/shard_map/pallas_call | solution.py:417
  105.6 0.0 collective-permute-done.14.refs_3_
  105.6 1.8 %shard_map.129 = (bf16[27,64,64]{2,1,0:T(8,128)(2,1)}, bf16[27,64,64]{2,1,0:T(8,128)(2,1)}, bf16[8,64,128]{2,1,0:T(8,128)(2,1)}) custom-call(s32[1,4]{1,0:T(1,128)S(1)} %add_bitcast_fusion.info_ref, bf16[16,4480]{1,0:T(8,128)(2,1)S(1)} %multiply_convert_fusion.refs_0_, bf16[16,4480]{1,0:T(8,128)(2,1)S(1)} %collective-permute-done.12.refs_1_, ...), custom_call_target="tpu_custom_call" | custom-call | flops 1 | bytes 1048576 | tf_op jit(solution)/shard_map/pallas_call | solution.py:417
  (20 shorter events, 0.1 us)
Async XLA Ops:
  1.5 9.3 %collective-permute-start = (bf16[64,512]{1,0:T(8,128)(2,1)S(1)}, bf16[64,512]{1,0:T(8,128)(2,1)S(1)}, u32[]{:S(2)}, u32[]{:S(2)}) collective-permute-start(bf16[64,512]{1,0:T(8,128)(2,1)S(1)} %get-tuple-element.107), channel_id=1, source_target_pairs={{0,4},{4,8},{8,12},{12,0},{1,5},{5,9},{9,13},{13,1},{2,6},{6,10},{... | collective-permute-start | bytes 196616 | tf_op jit(solution)/shard_map/ppermute | solution.py:430
  4.6 6.2 %collective-permute-start.1 = (bf16[64,512]{1,0:T(8,128)(2,1)S(1)}, bf16[64,512]{1,0:T(8,128)(2,1)S(1)}, u32[]{:S(2)}, u32[]{:S(2)}) collective-permute-start(bf16[64,512]{1,0:T(8,128)(2,1)S(1)} %get-tuple-element.106), channel_id=1, source_target_pairs={{0,12},{4,0},{8,4},{12,8},{1,13},{5,1},{9,5},{13,9},{2,14},{6,2},{... | collective-permute-start | bytes 196616 | tf_op jit(solution)/shard_map/ppermute | solution.py:430
  7.4 3.4 %copy-start.2 = (bf16[1,1536,64]{1,2,0:T(8,128)(2,1)S(1)}, bf16[1,1536,64]{1,2,0:T(8,128)(2,1)}, u32[]{:S(2)}) copy-start(bf16[1,1536,64]{1,2,0:T(8,128)(2,1)} %param.8) | copy-start | bytes 589828
  7.4 3.4 %copy-start.5 = (bf16[27,64,64]{2,1,0:T(8,128)(2,1)S(1)}, bf16[27,64,64]{2,1,0:T(8,128)(2,1)}, u32[]{:S(2)}) copy-start(bf16[27,64,64]{2,1,0:T(8,128)(2,1)} %weight_ref.13) | copy-start | bytes 663556
  7.4 3.4 %copy-start.6 = (s32[1,27,1536]{2,0,1:T(1,128)S(1)}, s32[1,27,1536]{2,0,1:T(1,128)}, u32[]{:S(2)}) copy-start(s32[1,27,1536]{2,0,1:T(1,128)} %param.9) | copy-start | bytes 497668
  10.9 0.8 copy-start.8
  22.5 8.8 %copy-start.4 = (bf16[27,64,64]{2,1,0:T(8,128)(2,1)S(1)}, bf16[27,64,64]{2,1,0:T(8,128)(2,1)}, u32[]{:S(2)}) copy-start(bf16[27,64,64]{2,1,0:T(8,128)(2,1)} %weight_ref.10) | copy-start | bytes 663556
  22.5 8.8 %copy-start.7 = (f32[64,1536]{1,0:T(8,128)S(1)}, f32[64,1536]{1,0:T(8,128)}, u32[]{:S(2)}) copy-start(f32[64,1536]{1,0:T(8,128)} %get-tuple-element.62.rows_ref) | copy-start | bytes 1179652
  22.5 8.1 %collective-permute-start.3 = (bf16[64,512]{1,0:T(8,128)(2,1)S(1)}, bf16[64,512]{1,0:T(8,128)(2,1)S(1)}, u32[]{:S(2)}, u32[]{:S(2)}) collective-permute-start(bf16[64,512]{1,0:T(8,128)(2,1)S(1)} %slice.23), channel_id=1, source_target_pairs={{0,12},{4,0},{8,4},{12,8},{1,13},{5,1},{9,5},{13,9},{2,14},{6,2},{... | collective-permute-start | bytes 196616 | tf_op jit(solution)/shard_map/ppermute | solution.py:430
  24.6 6.8 %collective-permute-start.2 = (bf16[128,512]{1,0:T(8,128)(2,1)S(1)}, bf16[128,512]{1,0:T(8,128)(2,1)S(1)}, u32[]{:S(2)}, u32[]{:S(2)}) collective-permute-start(bf16[128,512]{1,0:T(8,128)(2,1)S(1)} %get-tuple-element.61), channel_id=1, source_target_pairs={{0,4},{4,8},{8,12},{12,0},{1,5},{5,9},{9,13},{13,1},{2,6},{6,10},{... | collective-permute-start | bytes 393224 | tf_op jit(solution)/shard_map/ppermute | solution.py:430
  55.0 13.2 %collective-permute-start.4 = (bf16[128,512]{1,0:T(8,128)(2,1)S(1)}, bf16[128,512]{1,0:T(8,128)(2,1)S(1)}, u32[]{:S(2)}, u32[]{:S(2)}) collective-permute-start(bf16[128,512]{1,0:T(8,128)(2,1)S(1)} %get-tuple-element.64), channel_id=1, source_target_pairs={{0,12},{4,0},{8,4},{12,8},{1,13},{5,1},{9,5},{13,9},{2,14},{6,2},{... | collective-permute-start | bytes 393224 | tf_op jit(solution)/shard_map/ppermute | solution.py:430
  58.2 9.9 %collective-permute-start.5 = (bf16[64,512]{1,0:T(8,128)(2,1)S(1)}, bf16[64,512]{1,0:T(8,128)(2,1)S(1)}, u32[]{:S(2)}, u32[]{:S(2)}) collective-permute-start(bf16[64,512]{1,0:T(8,128)(2,1)S(1)} %get-tuple-element.65), channel_id=1, source_target_pairs={{0,4},{4,8},{8,12},{12,0},{1,5},{5,9},{9,13},{13,1},{2,6},{6,10},{... | collective-permute-start | bytes 196616 | tf_op jit(solution)/shard_map/ppermute | solution.py:430
  58.2 10.0 %copy-start = (bf16[8,64,128]{2,1,0:T(8,128)(2,1)S(1)}, bf16[8,64,128]{2,1,0:T(8,128)(2,1)}, u32[]{:S(2)}) copy-start(bf16[8,64,128]{2,1,0:T(8,128)(2,1)} %down_ref.3) | copy-start | bytes 393220
  58.2 10.0 %copy-start.1 = (bf16[1,384,128]{2,1,0:T(8,128)(2,1)S(1)}, bf16[1,384,128]{2,1,0:T(8,128)(2,1)}, u32[]{:S(2)}) copy-start(bf16[1,384,128]{2,1,0:T(8,128)(2,1)} %param.15) | copy-start | bytes 294916
  58.2 10.0 %copy-start.3 = (s32[1,8,384]{2,1,0:T(8,128)S(1)}, s32[1,8,384]{2,1,0:T(8,128)}, u32[]{:S(2)}) copy-start(s32[1,8,384]{2,1,0:T(8,128)} %param.10) | copy-start | bytes 36868
  71.7 8.8 %collective-permute-start.6 = (bf16[16,4480]{1,0:T(8,128)(2,1)S(1)}, bf16[16,4480]{1,0:T(8,128)(2,1)S(1)}, u32[]{:S(2)}, u32[]{:S(2)}) collective-permute-start(bf16[16,4480]{1,0:T(8,128)(2,1)S(1)} %get-tuple-element.74), channel_id=1, source_target_pairs={{0,1},{1,0},{2,3},{3,2},{4,5},{5,4},{6,7},{7,6},{8,9},{9,8},{10,11... | collective-permute-start | bytes 430088 | tf_op jit(solution)/shard_map/ppermute | solution.py:586
  71.8 8.7 %collective-permute-start.7 = (bf16[16,4480]{1,0:T(8,128)(2,1)S(1)}, bf16[16,4480]{1,0:T(8,128)(2,1)S(1)}, u32[]{:S(2)}, u32[]{:S(2)}) collective-permute-start(bf16[16,4480]{1,0:T(8,128)(2,1)S(1)} %get-tuple-element.75), channel_id=1, source_target_pairs={{0,2},{1,3},{2,0},{3,1},{4,6},{5,7},{6,4},{7,5},{8,10},{9,11},{10,... | collective-permute-start | bytes 430088 | tf_op jit(solution)/shard_map/ppermute | solution.py:586
  73.4 7.2 %collective-permute-start.8 = (bf16[16,4480]{1,0:T(8,128)(2,1)S(1)}, bf16[16,4480]{1,0:T(8,128)(2,1)S(1)}, u32[]{:S(2)}, u32[]{:S(2)}) collective-permute-start(bf16[16,4480]{1,0:T(8,128)(2,1)S(1)} %get-tuple-element.76), channel_id=1, source_target_pairs={{0,3},{1,2},{2,1},{3,0},{4,7},{5,6},{6,5},{7,4},{8,11},{9,10},{10,... | collective-permute-start | bytes 430088 | tf_op jit(solution)/shard_map/ppermute | solution.py:586
  80.7 12.7 %collective-permute-start.11 = (bf16[16,4480]{1,0:T(8,128)(2,1)S(1)}, bf16[16,4480]{1,0:T(8,128)(2,1)S(1)}, u32[]{:S(2)}, u32[]{:S(2)}) collective-permute-start(bf16[16,4480]{1,0:T(8,128)(2,1)S(1)} %add_convert_fusion), channel_id=1, source_target_pairs={{0,8},{4,12},{8,0},{12,4},{1,9},{5,13},{9,1},{13,5},{2,10},{6,14},... | collective-permute-start | bytes 430088 | tf_op jit(solution)/shard_map/ppermute | solution.py:430
  81.6 11.7 %collective-permute-start.10 = (bf16[16,6528]{1,0:T(8,128)(2,1)S(1)}, bf16[16,6528]{1,0:T(8,128)(2,1)S(1)}, u32[]{:S(2)}, u32[]{:S(2)}) collective-permute-start(bf16[16,6528]{1,0:T(8,128)(2,1)S(1)} %get-tuple-element.108), channel_id=1, source_target_pairs={{0,12},{4,0},{8,4},{12,8},{1,13},{5,1},{9,5},{13,9},{2,14},{6,2},{... | collective-permute-start | bytes 626696 | tf_op jit(solution)/shard_map/ppermute | solution.py:430
  84.6 13.2 %collective-permute-start.9 = (bf16[16,6528]{1,0:T(8,128)(2,1)S(1)}, bf16[16,6528]{1,0:T(8,128)(2,1)S(1)}, u32[]{:S(2)}, u32[]{:S(2)}) collective-permute-start(bf16[16,6528]{1,0:T(8,128)(2,1)S(1)} %get-tuple-element.109), channel_id=1, source_target_pairs={{0,4},{4,8},{8,12},{12,0},{1,5},{5,9},{9,13},{13,1},{2,6},{6,10},{... | collective-permute-start | bytes 626696 | tf_op jit(solution)/shard_map/ppermute | solution.py:430
  98.0 6.0 %collective-permute-start.12 = (bf16[16,4480]{1,0:T(8,128)(2,1)S(1)}, bf16[16,4480]{1,0:T(8,128)(2,1)S(1)}, u32[]{:S(2)}, u32[]{:S(2)}) collective-permute-start(bf16[16,4480]{1,0:T(8,128)(2,1)S(1)} %multiply_convert_fusion.refs_0_), channel_id=1, source_target_pairs={{0,1},{1,0},{2,3},{3,2},{4,5},{5,4},{6,7},{7,6},{8,9},{9,8},{10,11... | collective-permute-start | bytes 430088 | tf_op jit(solution)/shard_map/ppermute | solution.py:586
  98.0 6.2 %collective-permute-start.13 = (bf16[16,4480]{1,0:T(8,128)(2,1)S(1)}, bf16[16,4480]{1,0:T(8,128)(2,1)S(1)}, u32[]{:S(2)}, u32[]{:S(2)}) collective-permute-start(bf16[16,4480]{1,0:T(8,128)(2,1)S(1)} %multiply_convert_fusion.refs_0_), channel_id=1, source_target_pairs={{0,2},{1,3},{2,0},{3,1},{4,6},{5,7},{6,4},{7,5},{8,10},{9,11},{10,... | collective-permute-start | bytes 430088 | tf_op jit(solution)/shard_map/ppermute | solution.py:586
  104.2 1.4 %collective-permute-start.14 = (bf16[16,4480]{1,0:T(8,128)(2,1)S(1)}, bf16[16,4480]{1,0:T(8,128)(2,1)S(1)}, u32[]{:S(2)}, u32[]{:S(2)}) collective-permute-start(bf16[16,4480]{1,0:T(8,128)(2,1)S(1)} %collective-permute-done.13.refs_2_), channel_id=1, source_target_pairs={{0,1},{1,0},{2,3},{3,2},{4,5},{5,4},{6,7},{7,6},{8,9},{9,8},{10,11... | collective-permute-start | bytes 430088 | tf_op jit(solution)/shard_map/ppermute | solution.py:586
